TPU v7x, 32 devices: a whole 2x2x4 slice. The times are simulated.
32 devices in a mesh: grp: 2 (over x), tmpl: 8 (over z, y), tm: 2 (over core).
Axes of the slice: x: 2, y: 2, z: 4, core: 2. Of those that a mesh axis runs over, the one named last changes fastest.
Arguments:
- spectra: bfloat16 [1024, 4, 8192], P(('grp', 'tm', 'tmpl')), parts along dimension 0, may hold values from -6 to 6
- offsets: int32 [1024, 16], P(('grp', 'tm'), 'tmpl'), parts along dimension 0, may hold values from 0 to 1008
- fractions: float32 [4096], P(('grp', 'tmpl')), parts along dimension 0, may hold values from 0.1 to 0.9
- antenna: float32 [1024, 4], P('grp'), parts along dimension 0, may hold values from -2 to 2, as said below
- starts: int32 [64], P('grp'), parts along dimension 0, may hold values from 0 to 255
- durations: int32 [64], P('grp'), parts along dimension 0, may hold values from 48 to 256
Outputs:
- fstat_map: float32 [32, 32, 4096], P('tm', None, ('grp', 'tmpl')), parts along dimension 2
- loudest: float32 [64, 32], P(('grp', 'tm')), parts along dimension 0
There are 2 independent parts, one for each index of `grp`. A program takes and returns all parts, laid end to end along the dimension named above; each array names one. Nothing has to cross between parts.
Inputs may be any that keep to these rules, and one draw needn't show every extreme that they name: `antenna`: each detector's responses a and b turn once every 48 SFTs with magnitudes that vary from SFT to SFT.
All inputs are finite; a program needn't handle non-finite values.
Results may differ from a plain program's by a relative error of at most 0.0051.
Values may be sent and summed in bfloat16 or wider, within the bound.
No kernel may reach another device: no remote copies, remote signals or barrier semaphores. Data moves between devices by JAX's collectives and lax.ppermute only.
A program may use at most 128 MiB of HBM per device.

v0:
```python
import functools

import jax
import jax.numpy as jnp
from jax import lax
from jax.experimental import pallas as pl
from jax.experimental.pallas import tpu as pltpu
from jax.sharding import PartitionSpec as P

W = 16
LANES = 128
NT = (((1,), (1,)), ((), ()))


def iota(shape, axis):
    return lax.broadcasted_iota(jnp.int32, shape, axis)


def order(size, first):
    members = list(range(size))
    members[0], members[first] = first, 0
    return members


def hold_kernel(spec_ref, out_ref, sem):
    copy = pltpu.make_async_copy(spec_ref, out_ref, sem)
    copy.start()
    copy.wait()


def hold(spectra):
    return pl.pallas_call(
        hold_kernel,
        out_shape=jax.ShapeDtypeStruct(spectra.shape, spectra.dtype),
        in_specs=[pl.BlockSpec(memory_space=pl.ANY)],
        out_specs=pl.BlockSpec(memory_space=pltpu.VMEM),
        scratch_shapes=[pltpu.SemaphoreType.DMA],
        compiler_params=pltpu.CompilerParams(vmem_limit_bytes=8 * 1024 * 1024),
        cost_estimate=pl.CostEstimate(flops=0, bytes_accessed=4 * spectra.size, transcendentals=0),
        name="hold",
    )(spectra)


def pick_kernel(bands_in, bands_out, offset_ref, spec_ref, out_ref, place_ref, turn_ref):
    rows, _, bins = spec_ref.shape
    bands, blocks, _ = offset_ref.shape
    band_width = bins // bands
    groups = rows // 8
    chunks = band_width // LANES
    width = blocks * W
    first = lax.axis_index("tmpl").astype(jnp.int32) * rows
    columns = pl.ds(pl.multiple_of(first // LANES * LANES, LANES), LANES)
    offsets = jnp.concatenate([offset_ref[bands_in.index(band), :, columns] for band in range(bands)], axis=0).astype(jnp.float32)
    lane = iota(offsets.shape, 1)
    offsets = jnp.take_along_axis(offsets, (lane >> 2) + first & (LANES - 1), axis=1, mode="promise_in_bounds")
    offsets = jnp.concatenate([offsets, jnp.zeros((LANES - bands * blocks, LANES), jnp.float32)], axis=0)
    upright = jnp.transpose(offsets).astype(jnp.int32)
    lane = iota((32, LANES), 1)
    places = upright[0:32]
    for group in range(1, groups):
        turned = pltpu.roll(upright[group * 32 : group * 32 + 32], group * bands * blocks, 1)
        places = jnp.where(lane < group * bands * blocks, places, turned)
    lane = iota((8, LANES), 1)
    lane_group = lane // width
    source = lane_group * (bands * blocks) + lane // W % blocks
    for band in range(bands):
        for pair in range(4):
            place = jnp.take_along_axis(places[pair * 8 : pair * 8 + 8], source + band * blocks, axis=1, mode="promise_in_bounds")
            place_ref[band, pair] = place + ((lane & (W - 1)) + lane_group * band_width)

    def gather(band):
        for pair in range(4):
            place = place_ref[band, pair]
            lane_id = place & (LANES - 1)
            chosen = place >> 7
            tile = jnp.zeros((8, LANES), jnp.float32)
            for group in range(groups):
                for chunk in range(chunks):
                    columns = pl.ds(band * band_width + chunk * LANES, LANES)
                    values = spec_ref[pl.ds(group * 8 + pair * 2, 2), :, columns]
                    values = values.astype(jnp.float32).reshape(8, LANES)
                    moved = jnp.take_along_axis(values, lane_id, axis=1, mode="promise_in_bounds")
                    tile = jnp.where(chosen == group * chunks + chunk, moved, tile)
            turn_ref[band, pl.ds(pair * 8, 8), :] = tile

    def turn(band):
        parts = [turn_ref[band, pl.ds(part, 8, stride=4), :] for part in range(4)]
        tiles = []
        for group in range(groups):
            tile = jnp.zeros((8, LANES), jnp.float32)
            for part in range(4):
                amount = (part - group) * width % LANES
                turned = pltpu.roll(parts[part], amount, 1) if amount else parts[part]
                tile = jnp.where(lane_group == part, turned, tile)
            tiles.append(tile)
        return tiles

    tiles = {}
    for band in range(bands):
        gather(band)
        tiles[band] = turn(band)
    wanted = [tile for band in bands_out for tile in tiles[band]]
    for n in range(0, len(wanted), 2):
        out_ref[n * 8 : n * 8 + 16, :] = jnp.concatenate(wanted[n : n + 2], axis=0).astype(jnp.bfloat16)


def pick(offsets, spectra, bands_in, bands_out):
    rows, bands = spectra.shape[0], offsets.shape[0]
    out_rows = len(bands_out) * rows
    vmem = pl.BlockSpec(memory_space=pltpu.VMEM)
    return pl.pallas_call(
        functools.partial(pick_kernel, bands_in, bands_out),
        out_shape=jax.ShapeDtypeStruct((out_rows, LANES), jnp.bfloat16),
        in_specs=[vmem, vmem],
        out_specs=vmem,
        scratch_shapes=[
            pltpu.VMEM((bands, 4, 8, LANES), jnp.int32),
            pltpu.VMEM((bands, 32, LANES), jnp.float32),
        ],
        compiler_params=pltpu.CompilerParams(vmem_limit_bytes=8 * 1024 * 1024),
        cost_estimate=pl.CostEstimate(flops=10_000_000, bytes_accessed=2 * spectra.size, transcendentals=0),
        name="pick",
    )(offsets, spectra)


def split(values, count):
    parts = []
    for _ in range(count):
        part = values.astype(jnp.bfloat16)
        parts.append(part)
        values = values - part.astype(jnp.float32)
    return parts


def prepare_kernel(first, run, durations_ref, starts_ref, antenna_ref, fractions_ref, mask_ref, weigh_ref, coef_ref, kernel_ref):
    rows = starts_ref.shape[0]
    count = mask_ref.shape[0] // rows
    mine = lax.axis_index("tm").astype(jnp.int32) * count
    sfts = antenna_ref.shape[1]
    sft = iota((rows, sfts), 1)
    sft = jnp.where(sft // run == 0, sft + first * run, jnp.where(sft // run == first, sft - first * run, sft))
    start = starts_ref[:, 0:1]
    after = sft >= start
    for j in range(count):
        inside = after & (sft < start + durations_ref[mine + j])
        mask_ref[pl.ds(j * rows, rows), :] = jnp.where(inside, 1.0, 0.0).astype(jnp.bfloat16)
    antenna = jnp.concatenate([antenna_ref[...], jnp.zeros((4, sfts), jnp.float32)], axis=0)
    place = iota(antenna.shape, 1) // run
    after = pltpu.roll(antenna, sfts - first * run, 1)
    before = pltpu.roll(antenna, first * run, 1)
    antenna = jnp.where(place == 0, after, jnp.where(place == first, before, antenna))
    a1, a2, b1, b2 = (antenna[n : n + 1] for n in range(4))
    terms = jnp.concatenate([a1 * a1 + a2 * a2, b1 * b1 + b2 * b2, a1 * b1 + a2 * b2, jnp.zeros((5, sfts), jnp.float32)], axis=0)
    weights = sum(lax.dot_general(mask_ref[...], part, NT, preferred_element_type=jnp.float32) for part in split(terms, 3))
    wa, wb, wc = (weights[:, n : n + 1] for n in range(3))
    quarter = iota((rows * count, LANES), 1) // (LANES // 4)
    coef_ref[...] = jnp.where(quarter == 0, 1.0 / wa, jnp.where(quarter == 1, wa / (wa * wb - wc * wc), wc / wa))
    upright = jnp.transpose(jnp.concatenate([antenna, jnp.zeros((LANES - 8, sfts), jnp.float32)], axis=0))
    quarter = iota((sfts, LANES), 1) // (LANES // 4)
    early = jnp.where(quarter == 0, upright[:, 0:1], upright[:, 1:2])
    weigh_ref[...] = jnp.where(quarter < 2, early, jnp.where(quarter == 2, upright[:, 3:4], upright[:, 2:3]))
    fractions = fractions_ref[...]
    bin_id = iota((W, fractions.shape[1]), 0)
    distance = fractions + (W // 2 - 1) - bin_id.astype(jnp.float32)
    alternate = 1.0 - 2.0 * (bin_id % 2).astype(jnp.float32)
    kernel_ref[...] = (alternate * jnp.sin(jnp.pi * fractions) / (jnp.pi * distance)).astype(jnp.bfloat16)


def prepare(durations, starts, antenna, fractions, first, run, cores):
    count, rows, sfts = durations.shape[0] // cores, starts.shape[0], antenna.shape[0]
    vmem = pl.BlockSpec(memory_space=pltpu.VMEM)
    return pl.pallas_call(
        functools.partial(prepare_kernel, first, run),
        out_shape=(
            jax.ShapeDtypeStruct((count * rows, sfts), jnp.bfloat16),
            jax.ShapeDtypeStruct((sfts, LANES), jnp.float32),
            jax.ShapeDtypeStruct((count * rows, LANES), jnp.float32),
            jax.ShapeDtypeStruct((W, fractions.shape[0]), jnp.bfloat16),
        ),
        in_specs=[pl.BlockSpec(memory_space=pltpu.SMEM), vmem, vmem, vmem],
        out_specs=(vmem,) * 4,
        compiler_params=pltpu.CompilerParams(vmem_limit_bytes=16 * 1024 * 1024),
        cost_estimate=pl.CostEstimate(flops=100_000_000, bytes_accessed=4_000_000, transcendentals=0),
        name="prepare",
    )(durations, jnp.broadcast_to(starts[:, None], (rows, LANES)), antenna.T, fractions[None, :])


def statistic_kernel(windows_ref, mask_ref, weigh_ref, coef_ref, kernel_ref, map_ref, loudest_ref, block_ref, found_ref):
    templates = map_ref.shape[1]
    blocks = templates // LANES
    block_ref[...] = jnp.zeros_like(block_ref)
    for part in range(2):
        for c in range(4):
            for b in range(blocks):
                row, column = ((part * 4 + c) * blocks + b) * W, (c * blocks + b) * LANES
                block_ref[pl.ds(row, W), pl.ds(column, LANES)] = kernel_ref[:, b * LANES : (b + 1) * LANES]
    values = windows_ref[...].astype(jnp.float32)
    half, quarter = LANES // 2, LANES // 4
    weigh = weigh_ref[...]
    even = iota(weigh.shape, 1) // quarter % 2 == 0
    own = jnp.where(even, weigh, pltpu.roll(weigh, quarter, 1))
    other = jnp.where(even, pltpu.roll(weigh, LANES - quarter, 1), weigh)
    weighted = (own * values + other * pltpu.roll(values, half, 1)).astype(jnp.bfloat16)
    sums = jnp.dot(mask_ref[...], weighted, preferred_element_type=jnp.float32)
    sums = sums - jnp.where(iota(sums.shape, 1) < half, 0.0, coef_ref[...]) * pltpu.roll(sums, half, 1)
    parts = jnp.concatenate(split(sums, 2), axis=1)
    found_ref[...] = jnp.dot(parts, block_ref[...], preferred_element_type=jnp.float32)
    rows = map_ref.shape[0] // loudest_ref.shape[1]
    copies = loudest_ref.shape[0]
    per_step = LANES // rows
    for step in range(map_ref.shape[0] // LANES):
        here = pl.ds(step * LANES, LANES)
        scale_a = jnp.broadcast_to(coef_ref[here, 0:1], (LANES, LANES))
        scale_b = jnp.broadcast_to(coef_ref[here, quarter : quarter + 1], (LANES, LANES))
        best = None
        for b in range(blocks):
            ra, ia, rb, ib = (found_ref[here, pl.ds(c * templates + b * LANES, LANES)] for c in range(4))
            result = scale_a * (ra * ra + ia * ia) + scale_b * (rb * rb + ib * ib)
            map_ref[here, pl.ds(b * LANES, LANES)] = result
            best = result if best is None else jnp.maximum(best, result)
        best = jnp.max(jnp.transpose(best), axis=0, keepdims=True)
        for n in range(per_step):
            turned = best if n == 0 else pltpu.roll(best, LANES - n * rows, 1)
            for copy in range(copies):
                loudest_ref[copy, pl.ds(step * per_step + n, 1), :] = turned


def statistic(windows, mask, weigh, coef, kernel, rows, copies):
    count = mask.shape[0] // rows
    templates = kernel.shape[1]
    features = 4 * W * (templates // LANES)
    vmem = pl.BlockSpec(memory_space=pltpu.VMEM)
    return pl.pallas_call(
        statistic_kernel,
        out_shape=(
            jax.ShapeDtypeStruct((count * rows, templates), jnp.float32),
            jax.ShapeDtypeStruct((copies, count, LANES), jnp.float32),
        ),
        in_specs=[vmem] * 5,
        out_specs=(vmem, vmem),
        scratch_shapes=[
            pltpu.VMEM((2 * features, 4 * templates), jnp.bfloat16),
            pltpu.VMEM((count * rows, 4 * templates), jnp.float32),
        ],
        compiler_params=pltpu.CompilerParams(vmem_limit_bytes=16 * 1024 * 1024),
        cost_estimate=pl.CostEstimate(flops=400_000_000, bytes_accessed=4_000_000, transcendentals=0),
        name="statistic",
    )(windows, mask, weigh, coef, kernel)


def exchange(values, axis, members):
    return lax.all_to_all(values, axis, split_axis=0, concat_axis=0, axis_index_groups=[members], tiled=True)


def body(spectra, offsets, fractions, antenna, starts, durations):
    bands, cores = lax.axis_size("tmpl"), lax.axis_size("tm")
    sft_rows = spectra.shape[0]
    grid_size = starts.shape[0]
    my_rows = grid_size // cores
    by_band = order(bands, bands // 2)
    first = (cores - 1) * bands + bands // 2
    by_run = order(cores * bands, first)
    known = exchange(jnp.broadcast_to(offsets.T[None], (bands,) + offsets.T.shape), "tmpl", by_band)
    held, *late = lax.optimization_barrier((hold(spectra), durations, starts, antenna, fractions))
    prepared = prepare(*late, first, sft_rows, cores)
    held, *prepared = lax.optimization_barrier((held, *prepared))
    windows = pick(known, held, by_band, [run % bands for run in by_run])
    arrived = exchange(windows.reshape(cores * bands, sft_rows, LANES), ("tm", "tmpl"), by_run)
    fstat_map, loudest = statistic(arrived.reshape(-1, LANES), *prepared, grid_size, bands)
    loudest = jnp.max(exchange(loudest, "tmpl", by_band)[:, :, :grid_size], axis=0)
    return (fstat_map.reshape(my_rows, grid_size, -1), loudest)


def solution(mesh):
    in_specs = (
        P(("grp", "tm", "tmpl"), None, None),
        P(("grp", "tm"), "tmpl"),
        P(("grp", "tmpl")),
        P("grp", None),
        P("grp"),
        P("grp"),
    )
    out_specs = (P("tm", None, ("grp", "tmpl")), P(("grp", "tm"), None))
    return jax.shard_map(body, mesh=mesh, in_specs=in_specs, out_specs=out_specs, check_vma=False)
```

profile of v0, /device:TPU:0, one launch (start us, length us, event | category | flops | bytes accessed | tf_op | source)
XLA Modules:
  0.0 36.6 jit_solution(10334017071683066687)
XLA Ops:
  0.6 1.3 %broadcast_in_dim.6 = s32[8,2,256]{2,1,0:T(2,128)} broadcast(s32[2,256]{1,0:T(2,128)} %bitcast.10), dimensions={1,2} | broadcast | bytes 18432 | tf_op jit(solution)/shard_map/broadcast_in_dim | solution.py:263
  1.9 7.8 %all-to-all-start = ((s32[8,2,256]{2,1,0:T(2,128)}), s32[8,2,256]{2,1,0:T(2,128)S(1)}, u32[]{:S(2)}, u32[]{:S(2)}) async-start(s32[8,2,256]{2,1,0:T(2,128)} %broadcast_in_dim.6), calls=%async_computation | async-start | bytes 32768 | tf_op jit(solution)/shard_map/all_to_all | solution.py:252
  9.8 0.0 copy-start
  9.8 1.6 %copy-done = bf16[32,4,8192]{2,1,0:T(4,128)(2,1)S(1)} copy-done((bf16[32,4,8192]{2,1,0:T(4,128)(2,1)S(1)}, bf16[32,4,8192]{2,1,0:T(4,128)(2,1)}, u32[]{:S(2)}) %copy-start) | copy-done | bytes 2097176
  11.4 0.0 copy-start.4
  11.4 0.0 copy-start.1
  11.4 0.0 copy-start.2
  11.4 0.0 copy-start.3
  11.4 0.2 hold.1.spec_ref
  11.5 0.5 %copy-done.4 = s32[32]{0:T(128)S(1)} copy-done((s32[32]{0:T(128)S(1)}, s32[32]{0:T(128)}, u32[]{:S(2)}) %copy-start.4) | copy-done | bytes 152
  12.0 0.1 broadcast_in_dim.7.starts_ref
  12.1 0.0 copy-done.1
  12.1 0.0 copy-done.2
  12.1 0.0 copy-done.3
  12.1 1.9 %prepare.1 = (bf16[512,512]{1,0:T(8,128)(2,1)S(1)}, f32[512,128]{1,0:T(8,128)S(1)}, f32[512,128]{1,0:T(8,128)S(1)}, bf16[16,256]{1,0:T(8,128)(2,1)S(1)}) custom-call(s32[32]{0:T(128)S(1)} %copy-done.3, s32[32,128]{1,0:T(8,128)S(1)} %broadcast_in_dim.7.starts_ref, f32[4,512]{1,0:T(4,128)S(1)} %bitcast.8, f32[1,256]{1,0:T(1,128)S(1)} %bitcast.9), custom_call_target="tpu_custom_call" | custom-call | flops 100000000 | bytes 4000000 | tf_op jit(solution)/shard_map/prepare/pallas_call | solution.py:172
  14.0 0.0 all-to-all-done.offset_ref
  14.1 1.5 %pick.1 = bf16[512,128]{1,0:T(8,128)(2,1)S(1)} custom-call(s32[8,2,256]{2,1,0:T(2,128)S(1)} %all-to-all-done.offset_ref, bf16[32,4,8192]{2,1,0:T(4,128)(2,1)S(1)} %hold.1.spec_ref), custom_call_target="tpu_custom_call" | custom-call | flops 10000000 | bytes 2097152 | tf_op jit(solution)/shard_map/pick/pallas_call | solution.py:111
  15.6 9.9 %all_to_all.15 = bf16[16,32,128]{2,1,0:T(8,128)(2,1)S(1)} all-to-all(bf16[16,32,128]{2,1,0:T(8,128)(2,1)S(1)} %bitcast.6), channel_id=1, replica_groups={{9,2,4,6,8,10,12,14,1,3,5,7,0,11,13,15},{25,18,20,22,24,26,28,30,17,19,..., dimensions={0} | all-to-all | bytes 262144 | tf_op jit(solution)/shard_map/all_to_all | solution.py:252
  25.5 1.9 %statistic.1 = (f32[512,256]{1,0:T(8,128)}, f32[8,16,128]{2,1,0:T(8,128)S(1)}) custom-call(bf16[512,128]{1,0:T(8,128)(2,1)S(1)} %bitcast.7, bf16[512,512]{1,0:T(8,128)(2,1)S(1)} %get-tuple-element.28.mask_ref, f32[512,128]{1,0:T(8,128)S(1)} %get-tuple-element.29.weigh_ref, f32[512,128]{1,0:T(8,128)S(1)} %get-tuple-element.30.coef_ref, ...), custom_call_target="tpu_custom_call" | custom-call | flops 400000000 | bytes 4000000 | tf_op jit(solution)/shard_map/statistic/pallas_call | solution.py:233
  27.4 8.6 %all_to_all.16 = f32[8,16,128]{2,1,0:T(8,128)S(1)} all-to-all(f32[8,16,128]{2,1,0:T(8,128)S(1)} %get-tuple-element.33), channel_id=1, replica_groups={{8,2,4,6,0,10,12,14},{9,3,5,7,1,11,13,15},{24,18,20,22,16,26,28,30},{25..., dimensions={0} | all-to-all | bytes 131072 | tf_op jit(solution)/shard_map/all_to_all | solution.py:252
  36.0 0.6 %slice_reduce_fusion = f32[16,32]{1,0:T(8,128)} fusion(f32[8,16,128]{2,1,0:T(8,128)S(1)} %all_to_all.16), kind=kLoop, calls=%fused_computation | loop fusion | flops 3584 | bytes 18432 | tf_op jit(solution)/shard_map/reduce_max | solution.py:270
Async XLA Ops:
  1.9 12.1 %all-to-all-start = ((s32[8,2,256]{2,1,0:T(2,128)}), s32[8,2,256]{2,1,0:T(2,128)S(1)}, u32[]{:S(2)}, u32[]{:S(2)}) async-start(s32[8,2,256]{2,1,0:T(2,128)} %broadcast_in_dim.6), calls=%async_computation | async-start | bytes 32768 | tf_op jit(solution)/shard_map/all_to_all | solution.py:252
  9.8 1.6 %copy-start = (bf16[32,4,8192]{2,1,0:T(4,128)(2,1)S(1)}, bf16[32,4,8192]{2,1,0:T(4,128)(2,1)}, u32[]{:S(2)}) copy-start(bf16[32,4,8192]{2,1,0:T(4,128)(2,1)} %spec_ref.1) | copy-start | bytes 6291460
  11.4 0.7 %copy-start.4 = (s32[32]{0:T(128)S(1)}, s32[32]{0:T(128)}, u32[]{:S(2)}) copy-start(s32[32]{0:T(128)} %param.10) | copy-start | bytes 388
  11.4 0.7 %copy-start.1 = (f32[512,4]{0,1:T(4,128)S(1)}, f32[512,4]{0,1:T(4,128)}, u32[]{:S(2)}) copy-start(f32[512,4]{0,1:T(4,128)} %param.9) | copy-start | bytes 24580
  11.4 0.7 %copy-start.2 = (f32[256]{0:T(256)S(1)}, f32[256]{0:T(256)}, u32[]{:S(2)}) copy-start(f32[256]{0:T(256)} %param.8) | copy-start | bytes 3076
  11.4 0.7 %copy-start.3 = (s32[32]{0:T(128)S(1)}, s32[32]{0:T(128)}, u32[]{:S(2)}) copy-start(s32[32]{0:T(128)} %durations_ref) | copy-start | bytes 388
where the time goes:
time: 36.9 us; the launch traced here: 36.6 us
  blocking collectives  18.5 us (50%)
  starting transfers between devices  7.84 us (21%)
  Pallas kernels  5.51 us (15%)
  local copies, waits for them, and re-layouts  3.45 us (9%)
  between operations  0.67 us (2%)
  other arithmetic  0.61 us (2%)
    all_to_all x2, blocking collectives, exchange(): lax.all_to_all(values, axis, split_axis=0, concat_axis=0, axis_index_grou...  18.5 us
    all_to_all x1, starting transfers between devices, exchange(): lax.all_to_all(values, axis, split_axis=0, concat_axis=0, axis_index_grou...  7.84 us
    unnamed x10, local copies, waits for them, and re-layouts  2.09 us
    pallas_call x1, Pallas kernels, prepare(): pl.pallas_call(functools.partial(prepare_kernel, first, run), out_shape=(...  1.94 us
    pallas_call x1, Pallas kernels, statistic(): pl.pallas_call(statistic_kernel, out_shape=(jax.ShapeDtypeStruct((count *...  1.91 us
    pallas_call x1, Pallas kernels, pick(): pl.pallas_call(functools.partial(pick_kernel, bands_in, bands_out), out_s...  1.51 us
    broadcast_in_dim x1, local copies, waits for them, and re-layouts, body(): jnp.broadcast_to(offsets.T[None], (bands,) + offsets.T.shape)  1.29 us
  transfers between devices with their start and end apart: 1, of which 0 were waited for; matrix products, arithmetic and copies ran while one was open for 0% of the time, Pallas kernels for 6%

commit v1 on v0

--- a/solution.py
+++ b/solution.py
@@ -151,7 +151,9 @@
     antenna = jnp.where(place == 0, after, jnp.where(place == first, before, antenna))
     a1, a2, b1, b2 = (antenna[n : n + 1] for n in range(4))
     terms = jnp.concatenate([a1 * a1 + a2 * a2, b1 * b1 + b2 * b2, a1 * b1 + a2 * b2, jnp.zeros((5, sfts), jnp.float32)], axis=0)
-    weights = sum(lax.dot_general(mask_ref[...], part, NT, preferred_element_type=jnp.float32) for part in split(terms, 3))
+    parts = jnp.concatenate(split(terms, 3) + [jnp.zeros((LANES - 24, sfts), jnp.bfloat16)], axis=0)
+    weights = lax.dot_general(mask_ref[...], parts, NT, preferred_element_type=jnp.float32)
+    weights = weights + pltpu.roll(weights, LANES - 8, 1) + pltpu.roll(weights, LANES - 16, 1)
     wa, wb, wc = (weights[:, n : n + 1] for n in range(3))
     quarter = iota((rows * count, LANES), 1) // (LANES // 4)
     coef_ref[...] = jnp.where(quarter == 0, 1.0 / wa, jnp.where(quarter == 1, wa / (wa * wb - wc * wc), wc / wa))

time: 36.9 us -> 37 us (level)
  no operation moved by 1% of the time
where the time goes in v1:
time: 37 us; the launch traced here: 36.6 us
  blocking collectives  18.5 us (50%)
  starting transfers between devices  7.84 us (21%)
  Pallas kernels  5.53 us (15%)
  local copies, waits for them, and re-layouts  3.45 us (9%)
  between operations  0.67 us (2%)
  other arithmetic  0.61 us (2%)
    all_to_all x2, blocking collectives, exchange(): lax.all_to_all(values, axis, split_axis=0, concat_axis=0, axis_index_grou...  18.5 us
    all_to_all x1, starting transfers between devices, exchange(): lax.all_to_all(values, axis, split_axis=0, concat_axis=0, axis_index_grou...  7.84 us
    unnamed x10, local copies, waits for them, and re-layouts  2.09 us
    pallas_call x1, Pallas kernels, prepare(): pl.pallas_call(functools.partial(prepare_kernel, first, run), out_shape=(...  1.97 us
    pallas_call x1, Pallas kernels, statistic(): pl.pallas_call(statistic_kernel, out_shape=(jax.ShapeDtypeStruct((count *...  1.9 us
    pallas_call x1, Pallas kernels, pick(): pl.pallas_call(functools.partial(pick_kernel, bands_in, bands_out), out_s...  1.51 us
    broadcast_in_dim x1, local copies, waits for them, and re-layouts, body(): jnp.broadcast_to(offsets.T[None], (bands,) + offsets.T.shape)  1.29 us
  transfers between devices with their start and end apart: 1, of which 0 were waited for; matrix products, arithmetic and copies ran while one was open for 0% of the time, Pallas kernels for 6%

profile of v1, /device:TPU:0, one launch (start us, length us, event | category | flops | bytes accessed | tf_op | source)
XLA Modules:
  0.0 36.6 jit_solution(2267321213312014109)
XLA Ops:
  0.6 1.3 %broadcast_in_dim.6 = s32[8,2,256]{2,1,0:T(2,128)} broadcast(s32[2,256]{1,0:T(2,128)} %bitcast.10), dimensions={1,2} | broadcast | bytes 18432 | tf_op jit(solution)/shard_map/broadcast_in_dim | solution.py:265
  1.9 7.8 %all-to-all-start = ((s32[8,2,256]{2,1,0:T(2,128)}), s32[8,2,256]{2,1,0:T(2,128)S(1)}, u32[]{:S(2)}, u32[]{:S(2)}) async-start(s32[8,2,256]{2,1,0:T(2,128)} %broadcast_in_dim.6), calls=%async_computation | async-start | bytes 32768 | tf_op jit(solution)/shard_map/all_to_all | solution.py:254
  9.8 0.0 copy-start
  9.8 1.6 %copy-done = bf16[32,4,8192]{2,1,0:T(4,128)(2,1)S(1)} copy-done((bf16[32,4,8192]{2,1,0:T(4,128)(2,1)S(1)}, bf16[32,4,8192]{2,1,0:T(4,128)(2,1)}, u32[]{:S(2)}) %copy-start) | copy-done | bytes 2097176
  11.4 0.0 copy-start.4
  11.4 0.0 copy-start.1
  11.4 0.0 copy-start.2
  11.4 0.0 copy-start.3
  11.4 0.2 hold.1.spec_ref
  11.5 0.5 %copy-done.4 = s32[32]{0:T(128)S(1)} copy-done((s32[32]{0:T(128)S(1)}, s32[32]{0:T(128)}, u32[]{:S(2)}) %copy-start.4) | copy-done | bytes 152
  12.0 0.1 broadcast_in_dim.7.starts_ref
  12.1 0.0 copy-done.1
  12.1 0.0 copy-done.2
  12.1 0.0 copy-done.3
  12.1 2.0 %prepare.1 = (bf16[512,512]{1,0:T(8,128)(2,1)S(1)}, f32[512,128]{1,0:T(8,128)S(1)}, f32[512,128]{1,0:T(8,128)S(1)}, bf16[16,256]{1,0:T(8,128)(2,1)S(1)}) custom-call(s32[32]{0:T(128)S(1)} %copy-done.3, s32[32,128]{1,0:T(8,128)S(1)} %broadcast_in_dim.7.starts_ref, f32[4,512]{1,0:T(4,128)S(1)} %bitcast.8, f32[1,256]{1,0:T(1,128)S(1)} %bitcast.9), custom_call_target="tpu_custom_call" | custom-call | flops 100000000 | bytes 4000000 | tf_op jit(solution)/shard_map/prepare/pallas_call | solution.py:174
  14.1 0.0 all-to-all-done.offset_ref
  14.1 1.5 %pick.1 = bf16[512,128]{1,0:T(8,128)(2,1)S(1)} custom-call(s32[8,2,256]{2,1,0:T(2,128)S(1)} %all-to-all-done.offset_ref, bf16[32,4,8192]{2,1,0:T(4,128)(2,1)S(1)} %hold.1.spec_ref), custom_call_target="tpu_custom_call" | custom-call | flops 10000000 | bytes 2097152 | tf_op jit(solution)/shard_map/pick/pallas_call | solution.py:111
  15.6 9.9 %all_to_all.15 = bf16[16,32,128]{2,1,0:T(8,128)(2,1)S(1)} all-to-all(bf16[16,32,128]{2,1,0:T(8,128)(2,1)S(1)} %bitcast.6), channel_id=1, replica_groups={{9,2,4,6,8,10,12,14,1,3,5,7,0,11,13,15},{25,18,20,22,24,26,28,30,17,19,..., dimensions={0} | all-to-all | bytes 262144 | tf_op jit(solution)/shard_map/all_to_all | solution.py:254
  25.5 1.9 %statistic.1 = (f32[512,256]{1,0:T(8,128)}, f32[8,16,128]{2,1,0:T(8,128)S(1)}) custom-call(bf16[512,128]{1,0:T(8,128)(2,1)S(1)} %bitcast.7, bf16[512,512]{1,0:T(8,128)(2,1)S(1)} %get-tuple-element.28.mask_ref, f32[512,128]{1,0:T(8,128)S(1)} %get-tuple-element.29.weigh_ref, f32[512,128]{1,0:T(8,128)S(1)} %get-tuple-element.30.coef_ref, ...), custom_call_target="tpu_custom_call" | custom-call | flops 400000000 | bytes 4000000 | tf_op jit(solution)/shard_map/statistic/pallas_call | solution.py:235
  27.4 8.6 %all_to_all.16 = f32[8,16,128]{2,1,0:T(8,128)S(1)} all-to-all(f32[8,16,128]{2,1,0:T(8,128)S(1)} %get-tuple-element.33), channel_id=1, replica_groups={{8,2,4,6,0,10,12,14},{9,3,5,7,1,11,13,15},{24,18,20,22,16,26,28,30},{25..., dimensions={0} | all-to-all | bytes 131072 | tf_op jit(solution)/shard_map/all_to_all | solution.py:254
  36.0 0.6 %slice_reduce_fusion = f32[16,32]{1,0:T(8,128)} fusion(f32[8,16,128]{2,1,0:T(8,128)S(1)} %all_to_all.16), kind=kLoop, calls=%fused_computation | loop fusion | flops 3584 | bytes 18432 | tf_op jit(solution)/shard_map/reduce_max | solution.py:272
Async XLA Ops:
  1.9 12.2 %all-to-all-start = ((s32[8,2,256]{2,1,0:T(2,128)}), s32[8,2,256]{2,1,0:T(2,128)S(1)}, u32[]{:S(2)}, u32[]{:S(2)}) async-start(s32[8,2,256]{2,1,0:T(2,128)} %broadcast_in_dim.6), calls=%async_computation | async-start | bytes 32768 | tf_op jit(solution)/shard_map/all_to_all | solution.py:254
  9.8 1.6 %copy-start = (bf16[32,4,8192]{2,1,0:T(4,128)(2,1)S(1)}, bf16[32,4,8192]{2,1,0:T(4,128)(2,1)}, u32[]{:S(2)}) copy-start(bf16[32,4,8192]{2,1,0:T(4,128)(2,1)} %spec_ref.1) | copy-start | bytes 6291460
  11.4 0.7 %copy-start.4 = (s32[32]{0:T(128)S(1)}, s32[32]{0:T(128)}, u32[]{:S(2)}) copy-start(s32[32]{0:T(128)} %param.10) | copy-start | bytes 388
  11.4 0.7 %copy-start.1 = (f32[512,4]{0,1:T(4,128)S(1)}, f32[512,4]{0,1:T(4,128)}, u32[]{:S(2)}) copy-start(f32[512,4]{0,1:T(4,128)} %param.9) | copy-start | bytes 24580
  11.4 0.7 %copy-start.2 = (f32[256]{0:T(256)S(1)}, f32[256]{0:T(256)}, u32[]{:S(2)}) copy-start(f32[256]{0:T(256)} %param.8) | copy-start | bytes 3076
  11.4 0.7 %copy-start.3 = (s32[32]{0:T(128)S(1)}, s32[32]{0:T(128)}, u32[]{:S(2)}) copy-start(s32[32]{0:T(128)} %durations_ref) | copy-start | bytes 388

commit v2 on v0

--- a/solution.py
+++ b/solution.py
@@ -151,14 +151,16 @@
     antenna = jnp.where(place == 0, after, jnp.where(place == first, before, antenna))
     a1, a2, b1, b2 = (antenna[n : n + 1] for n in range(4))
     terms = jnp.concatenate([a1 * a1 + a2 * a2, b1 * b1 + b2 * b2, a1 * b1 + a2 * b2, jnp.zeros((5, sfts), jnp.float32)], axis=0)
-    weights = sum(lax.dot_general(mask_ref[...], part, NT, preferred_element_type=jnp.float32) for part in split(terms, 3))
-    wa, wb, wc = (weights[:, n : n + 1] for n in range(3))
-    quarter = iota((rows * count, LANES), 1) // (LANES // 4)
-    coef_ref[...] = jnp.where(quarter == 0, 1.0 / wa, jnp.where(quarter == 1, wa / (wa * wb - wc * wc), wc / wa))
-    upright = jnp.transpose(jnp.concatenate([antenna, jnp.zeros((LANES - 8, sfts), jnp.float32)], axis=0))
-    quarter = iota((sfts, LANES), 1) // (LANES // 4)
-    early = jnp.where(quarter == 0, upright[:, 0:1], upright[:, 1:2])
-    weigh_ref[...] = jnp.where(quarter < 2, early, jnp.where(quarter == 2, upright[:, 3:4], upright[:, 2:3]))
+    sums = lax.dot_general(jnp.concatenate(split(terms, 3), axis=0), mask_ref[...], NT, preferred_element_type=jnp.float32)
+    sums = sums[0:8] + sums[8:16] + sums[16:24]
+    wa, wb, wc = (sums[n : n + 1] for n in range(3))
+
+    def quarters(*factors):
+        shape = (LANES // 4, factors[0].shape[1])
+        return jnp.transpose(jnp.concatenate([jnp.broadcast_to(factor, shape) for factor in factors], axis=0))
+
+    coef_ref[...] = quarters(1.0 / wa, wa / (wa * wb - wc * wc), wc / wa, wc / wa)
+    weigh_ref[...] = quarters(a1, a2, b2, b1)
     fractions = fractions_ref[...]
     bin_id = iota((W, fractions.shape[1]), 0)
     distance = fractions + (W // 2 - 1) - bin_id.astype(jnp.float32)

time: 36.9 us -> 36.2 us (0.981)
  Pallas kernels: 5.51 us -> 4.72 us
  blocking collectives: 18.5 us -> 17.8 us
  waiting for transfers between devices: 0.01 us -> 0.7 us
    pallas_call x1, Pallas kernels: 1.94 us -> 1.16 us  [prepare(): pl.pallas_call(functools.partial(prepare_kernel, first, run), out_shape=(...]
    all_to_all x1, waiting for transfers between devices: 0.01 us -> 0.7 us  [exchange(): lax.all_to_all(values, axis, split_axis=0, concat_axis=0, axis_index_grou...]
    all_to_all x2, blocking collectives: 18.5 us -> 17.8 us  [exchange(): lax.all_to_all(values, axis, split_axis=0, concat_axis=0, axis_index_grou...]
  transfers between devices with their start and end apart: 1 -> 1, of which waited for: 0 -> 1; matrix products, arithmetic and copies ran while one was open for 0% -> 0% of each run, Pallas kernels for 6% -> 4%
where the time goes in v2:
time: 36.2 us; the launch traced here: 35.8 us
  blocking collectives  17.8 us (49%)
  starting transfers between devices  7.84 us (22%)
  Pallas kernels  4.72 us (13%)
  local copies, waits for them, and re-layouts  3.45 us (10%)
  waiting for transfers between devices  0.7 us (2%)
  between operations  0.66 us (2%)
  other arithmetic  0.61 us (2%)
    all_to_all x2, blocking collectives, exchange(): lax.all_to_all(values, axis, split_axis=0, concat_axis=0, axis_index_grou...  17.8 us
    all_to_all x1, starting transfers between devices, exchange(): lax.all_to_all(values, axis, split_axis=0, concat_axis=0, axis_index_grou...  7.84 us
    unnamed x10, local copies, waits for them, and re-layouts  2.09 us
    pallas_call x1, Pallas kernels, statistic(): pl.pallas_call(statistic_kernel, out_shape=(jax.ShapeDtypeStruct((count *...  1.91 us
    pallas_call x1, Pallas kernels, pick(): pl.pallas_call(functools.partial(pick_kernel, bands_in, bands_out), out_s...  1.5 us
    broadcast_in_dim x1, local copies, waits for them, and re-layouts, body(): jnp.broadcast_to(offsets.T[None], (bands,) + offsets.T.shape)  1.29 us
    pallas_call x1, Pallas kernels, prepare(): pl.pallas_call(functools.partial(prepare_kernel, first, run), out_shape=(...  1.16 us
  transfers between devices with their start and end apart: 1, of which 1 were waited for; matrix products, arithmetic and copies ran while one was open for 0% of the time, Pallas kernels for 4%

profile of v2, /device:TPU:0, one launch (start us, length us, event | category | flops | bytes accessed | tf_op | source)
XLA Modules:
  0.0 35.8 jit_solution(45227952735091206)
XLA Ops:
  0.6 1.3 %broadcast_in_dim.6 = s32[8,2,256]{2,1,0:T(2,128)} broadcast(s32[2,256]{1,0:T(2,128)} %bitcast.10), dimensions={1,2} | broadcast | bytes 18432 | tf_op jit(solution)/shard_map/broadcast_in_dim | solution.py:265
  1.9 7.8 %all-to-all-start = ((s32[8,2,256]{2,1,0:T(2,128)}), s32[8,2,256]{2,1,0:T(2,128)S(1)}, u32[]{:S(2)}, u32[]{:S(2)}) async-start(s32[8,2,256]{2,1,0:T(2,128)} %broadcast_in_dim.6), calls=%async_computation | async-start | bytes 32768 | tf_op jit(solution)/shard_map/all_to_all | solution.py:254
  9.8 0.0 copy-start
  9.8 1.6 %copy-done = bf16[32,4,8192]{2,1,0:T(4,128)(2,1)S(1)} copy-done((bf16[32,4,8192]{2,1,0:T(4,128)(2,1)S(1)}, bf16[32,4,8192]{2,1,0:T(4,128)(2,1)}, u32[]{:S(2)}) %copy-start) | copy-done | bytes 2097176
  11.4 0.0 copy-start.4
  11.4 0.0 copy-start.1
  11.4 0.0 copy-start.2
  11.4 0.0 copy-start.3
  11.4 0.2 hold.1.spec_ref
  11.5 0.5 %copy-done.4 = s32[32]{0:T(128)S(1)} copy-done((s32[32]{0:T(128)S(1)}, s32[32]{0:T(128)}, u32[]{:S(2)}) %copy-start.4) | copy-done | bytes 152
  12.0 0.1 broadcast_in_dim.7.starts_ref
  12.1 0.0 copy-done.1
  12.1 0.0 copy-done.2
  12.1 0.0 copy-done.3
  12.1 1.2 %prepare.1 = (bf16[512,512]{1,0:T(8,128)(2,1)S(1)}, f32[512,128]{1,0:T(8,128)S(1)}, f32[512,128]{1,0:T(8,128)S(1)}, bf16[16,256]{1,0:T(8,128)(2,1)S(1)}) custom-call(s32[32]{0:T(128)S(1)} %copy-done.3, s32[32,128]{1,0:T(8,128)S(1)} %broadcast_in_dim.7.starts_ref, f32[4,512]{1,0:T(4,128)S(1)} %bitcast.8, f32[1,256]{1,0:T(1,128)S(1)} %bitcast.9), custom_call_target="tpu_custom_call" | custom-call | flops 100000000 | bytes 4000000 | tf_op jit(solution)/shard_map/prepare/pallas_call | solution.py:174
  13.3 0.7 %all-to-all-done.offset_ref = s32[8,2,256]{2,1,0:T(2,128)S(1)} async-done(((s32[8,2,256]{2,1,0:T(2,128)}), s32[8,2,256]{2,1,0:T(2,128)S(1)}, u32[]{:S(2)}, u32[]{:S(2)}) %all-to-all-start) | async-done | bytes 16416 | tf_op jit(solution)/shard_map/all_to_all | solution.py:254
  14.0 1.5 %pick.1 = bf16[512,128]{1,0:T(8,128)(2,1)S(1)} custom-call(s32[8,2,256]{2,1,0:T(2,128)S(1)} %all-to-all-done.offset_ref, bf16[32,4,8192]{2,1,0:T(4,128)(2,1)S(1)} %hold.1.spec_ref), custom_call_target="tpu_custom_call" | custom-call | flops 10000000 | bytes 2097152 | tf_op jit(solution)/shard_map/pick/pallas_call | solution.py:111
  15.5 9.3 %all_to_all.15 = bf16[16,32,128]{2,1,0:T(8,128)(2,1)S(1)} all-to-all(bf16[16,32,128]{2,1,0:T(8,128)(2,1)S(1)} %bitcast.6), channel_id=1, replica_groups={{9,2,4,6,8,10,12,14,1,3,5,7,0,11,13,15},{25,18,20,22,24,26,28,30,17,19,..., dimensions={0} | all-to-all | bytes 262144 | tf_op jit(solution)/shard_map/all_to_all | solution.py:254
  24.7 1.9 %statistic.1 = (f32[512,256]{1,0:T(8,128)}, f32[8,16,128]{2,1,0:T(8,128)S(1)}) custom-call(bf16[512,128]{1,0:T(8,128)(2,1)S(1)} %bitcast.7, bf16[512,512]{1,0:T(8,128)(2,1)S(1)} %get-tuple-element.28.mask_ref, f32[512,128]{1,0:T(8,128)S(1)} %get-tuple-element.29.weigh_ref, f32[512,128]{1,0:T(8,128)S(1)} %get-tuple-element.30.coef_ref, ...), custom_call_target="tpu_custom_call" | custom-call | flops 400000000 | bytes 4000000 | tf_op jit(solution)/shard_map/statistic/pallas_call | solution.py:235
  26.6 8.6 %all_to_all.16 = f32[8,16,128]{2,1,0:T(8,128)S(1)} all-to-all(f32[8,16,128]{2,1,0:T(8,128)S(1)} %get-tuple-element.33), channel_id=1, replica_groups={{8,2,4,6,0,10,12,14},{9,3,5,7,1,11,13,15},{24,18,20,22,16,26,28,30},{25..., dimensions={0} | all-to-all | bytes 131072 | tf_op jit(solution)/shard_map/all_to_all | solution.py:254
  35.2 0.6 %slice_reduce_fusion = f32[16,32]{1,0:T(8,128)} fusion(f32[8,16,128]{2,1,0:T(8,128)S(1)} %all_to_all.16), kind=kLoop, calls=%fused_computation | loop fusion | flops 3584 | bytes 18432 | tf_op jit(solution)/shard_map/reduce_max | solution.py:272
Async XLA Ops:
  1.9 12.0 %all-to-all-start = ((s32[8,2,256]{2,1,0:T(2,128)}), s32[8,2,256]{2,1,0:T(2,128)S(1)}, u32[]{:S(2)}, u32[]{:S(2)}) async-start(s32[8,2,256]{2,1,0:T(2,128)} %broadcast_in_dim.6), calls=%async_computation | async-start | bytes 32768 | tf_op jit(solution)/shard_map/all_to_all | solution.py:254
  9.8 1.6 %copy-start = (bf16[32,4,8192]{2,1,0:T(4,128)(2,1)S(1)}, bf16[32,4,8192]{2,1,0:T(4,128)(2,1)}, u32[]{:S(2)}) copy-start(bf16[32,4,8192]{2,1,0:T(4,128)(2,1)} %spec_ref.1) | copy-start | bytes 6291460
  11.4 0.7 %copy-start.4 = (s32[32]{0:T(128)S(1)}, s32[32]{0:T(128)}, u32[]{:S(2)}) copy-start(s32[32]{0:T(128)} %param.10) | copy-start | bytes 388
  11.4 0.7 %copy-start.1 = (f32[512,4]{0,1:T(4,128)S(1)}, f32[512,4]{0,1:T(4,128)}, u32[]{:S(2)}) copy-start(f32[512,4]{0,1:T(4,128)} %param.9) | copy-start | bytes 24580
  11.4 0.7 %copy-start.2 = (f32[256]{0:T(256)S(1)}, f32[256]{0:T(256)}, u32[]{:S(2)}) copy-start(f32[256]{0:T(256)} %param.8) | copy-start | bytes 3076
  11.4 0.7 %copy-start.3 = (s32[32]{0:T(128)S(1)}, s32[32]{0:T(128)}, u32[]{:S(2)}) copy-start(s32[32]{0:T(128)} %durations_ref) | copy-start | bytes 388

commit v3 on v2

--- a/solution.py
+++ b/solution.py
@@ -187,7 +187,7 @@
     )(durations, jnp.broadcast_to(starts[:, None], (rows, LANES)), antenna.T, fractions[None, :])
 
 
-def statistic_kernel(windows_ref, mask_ref, weigh_ref, coef_ref, kernel_ref, map_ref, loudest_ref, block_ref, found_ref):
+def statistic_kernel(windows_ref, mask_ref, weigh_ref, coef_ref, kernel_ref, map_ref, loudest_ref, block_ref, found_ref, tile_ref, sems):
     templates = map_ref.shape[1]
     blocks = templates // LANES
     block_ref[...] = jnp.zeros_like(block_ref)
@@ -210,6 +210,7 @@
     rows = map_ref.shape[0] // loudest_ref.shape[1]
     copies = loudest_ref.shape[0]
     per_step = LANES // rows
+    leaving = []
     for step in range(map_ref.shape[0] // LANES):
         here = pl.ds(step * LANES, LANES)
         scale_a = jnp.broadcast_to(coef_ref[here, 0:1], (LANES, LANES))
@@ -218,13 +219,18 @@
         for b in range(blocks):
             ra, ia, rb, ib = (found_ref[here, pl.ds(c * templates + b * LANES, LANES)] for c in range(4))
             result = scale_a * (ra * ra + ia * ia) + scale_b * (rb * rb + ib * ib)
-            map_ref[here, pl.ds(b * LANES, LANES)] = result
+            tile_ref[here, pl.ds(b * LANES, LANES)] = result
             best = result if best is None else jnp.maximum(best, result)
+        leaving.append(pltpu.make_async_copy(tile_ref.at[here, :], map_ref.at[here, :], sems.at[step]))
+        leaving[-1].start()
         best = jnp.max(jnp.transpose(best), axis=0, keepdims=True)
         for n in range(per_step):
             turned = best if n == 0 else pltpu.roll(best, LANES - n * rows, 1)
-            for copy in range(copies):
-                loudest_ref[copy, pl.ds(step * per_step + n, 1), :] = turned
+            loudest_ref[0, pl.ds(step * per_step + n, 1), :] = turned
+    for copy in range(1, copies):
+        loudest_ref[copy] = loudest_ref[0]
+    for copy in leaving:
+        copy.wait()
 
 
 def statistic(windows, mask, weigh, coef, kernel, rows, copies):
@@ -239,10 +245,12 @@
             jax.ShapeDtypeStruct((copies, count, LANES), jnp.float32),
         ),
         in_specs=[vmem] * 5,
-        out_specs=(vmem, vmem),
+        out_specs=(pl.BlockSpec(memory_space=pl.ANY), vmem),
         scratch_shapes=[
             pltpu.VMEM((2 * features, 4 * templates), jnp.bfloat16),
             pltpu.VMEM((count * rows, 4 * templates), jnp.float32),
+            pltpu.VMEM((count * rows, templates), jnp.float32),
+            pltpu.SemaphoreType.DMA((count * rows // LANES,)),
         ],
         compiler_params=pltpu.CompilerParams(vmem_limit_bytes=16 * 1024 * 1024),
         cost_estimate=pl.CostEstimate(flops=400_000_000, bytes_accessed=4_000_000, transcendentals=0),

time: 36.2 us -> 36.1 us (level)
  no operation moved by 1% of the time
where the time goes in v3:
time: 36.1 us; the launch traced here: 35.7 us
  blocking collectives  17.9 us (50%)
  starting transfers between devices  7.84 us (22%)
  Pallas kernels  4.62 us (13%)
  local copies, waits for them, and re-layouts  3.45 us (10%)
  waiting for transfers between devices  0.7 us (2%)
  between operations  0.67 us (2%)
  other arithmetic  0.61 us (2%)
    all_to_all x2, blocking collectives, exchange(): lax.all_to_all(values, axis, split_axis=0, concat_axis=0, axis_index_grou...  17.9 us
    all_to_all x1, starting transfers between devices, exchange(): lax.all_to_all(values, axis, split_axis=0, concat_axis=0, axis_index_grou...  7.84 us
    unnamed x10, local copies, waits for them, and re-layouts  2.09 us
    pallas_call x1, Pallas kernels, statistic(): pl.pallas_call(statistic_kernel, out_shape=(jax.ShapeDtypeStruct((count *...  1.8 us
    pallas_call x1, Pallas kernels, pick(): pl.pallas_call(functools.partial(pick_kernel, bands_in, bands_out), out_s...  1.5 us
    broadcast_in_dim x1, local copies, waits for them, and re-layouts, body(): jnp.broadcast_to(offsets.T[None], (bands,) + offsets.T.shape)  1.29 us
    pallas_call x1, Pallas kernels, prepare(): pl.pallas_call(functools.partial(prepare_kernel, first, run), out_shape=(...  1.16 us
  transfers between devices with their start and end apart: 1, of which 1 were waited for; matrix products, arithmetic and copies ran while one was open for 0% of the time, Pallas kernels for 4%

profile of v3, /device:TPU:0, one launch (start us, length us, event | category | flops | bytes accessed | tf_op | source)
XLA Modules:
  0.0 35.7 jit_solution(1175099404984687349)
XLA Ops:
  0.6 1.3 %broadcast_in_dim.6 = s32[8,2,256]{2,1,0:T(2,128)} broadcast(s32[2,256]{1,0:T(2,128)} %bitcast.10), dimensions={1,2} | broadcast | bytes 18432 | tf_op jit(solution)/shard_map/broadcast_in_dim | solution.py:273
  1.9 7.8 %all-to-all-start = ((s32[8,2,256]{2,1,0:T(2,128)}), s32[8,2,256]{2,1,0:T(2,128)S(1)}, u32[]{:S(2)}, u32[]{:S(2)}) async-start(s32[8,2,256]{2,1,0:T(2,128)} %broadcast_in_dim.6), calls=%async_computation | async-start | bytes 32768 | tf_op jit(solution)/shard_map/all_to_all | solution.py:262
  9.8 0.0 copy-start
  9.8 1.6 %copy-done = bf16[32,4,8192]{2,1,0:T(4,128)(2,1)S(1)} copy-done((bf16[32,4,8192]{2,1,0:T(4,128)(2,1)S(1)}, bf16[32,4,8192]{2,1,0:T(4,128)(2,1)}, u32[]{:S(2)}) %copy-start) | copy-done | bytes 2097176
  11.4 0.0 copy-start.4
  11.4 0.0 copy-start.1
  11.4 0.0 copy-start.2
  11.4 0.0 copy-start.3
  11.4 0.2 hold.1.spec_ref
  11.5 0.5 %copy-done.4 = s32[32]{0:T(128)S(1)} copy-done((s32[32]{0:T(128)S(1)}, s32[32]{0:T(128)}, u32[]{:S(2)}) %copy-start.4) | copy-done | bytes 152
  12.0 0.1 broadcast_in_dim.7.starts_ref
  12.1 0.0 copy-done.1
  12.1 0.0 copy-done.2
  12.1 0.0 copy-done.3
  12.1 1.2 %prepare.1 = (bf16[512,512]{1,0:T(8,128)(2,1)S(1)}, f32[512,128]{1,0:T(8,128)S(1)}, f32[512,128]{1,0:T(8,128)S(1)}, bf16[16,256]{1,0:T(8,128)(2,1)S(1)}) custom-call(s32[32]{0:T(128)S(1)} %copy-done.3, s32[32,128]{1,0:T(8,128)S(1)} %broadcast_in_dim.7.starts_ref, f32[4,512]{1,0:T(4,128)S(1)} %bitcast.8, f32[1,256]{1,0:T(1,128)S(1)} %bitcast.9), custom_call_target="tpu_custom_call" | custom-call | flops 100000000 | bytes 4000000 | tf_op jit(solution)/shard_map/prepare/pallas_call | solution.py:174
  13.3 0.7 %all-to-all-done.offset_ref = s32[8,2,256]{2,1,0:T(2,128)S(1)} async-done(((s32[8,2,256]{2,1,0:T(2,128)}), s32[8,2,256]{2,1,0:T(2,128)S(1)}, u32[]{:S(2)}, u32[]{:S(2)}) %all-to-all-start) | async-done | bytes 16416 | tf_op jit(solution)/shard_map/all_to_all | solution.py:262
  14.0 1.5 %pick.1 = bf16[512,128]{1,0:T(8,128)(2,1)S(1)} custom-call(s32[8,2,256]{2,1,0:T(2,128)S(1)} %all-to-all-done.offset_ref, bf16[32,4,8192]{2,1,0:T(4,128)(2,1)S(1)} %hold.1.spec_ref), custom_call_target="tpu_custom_call" | custom-call | flops 10000000 | bytes 2097152 | tf_op jit(solution)/shard_map/pick/pallas_call | solution.py:111
  15.5 9.3 %all_to_all.15 = bf16[16,32,128]{2,1,0:T(8,128)(2,1)S(1)} all-to-all(bf16[16,32,128]{2,1,0:T(8,128)(2,1)S(1)} %bitcast.6), channel_id=1, replica_groups={{9,2,4,6,8,10,12,14,1,3,5,7,0,11,13,15},{25,18,20,22,24,26,28,30,17,19,..., dimensions={0} | all-to-all | bytes 262144 | tf_op jit(solution)/shard_map/all_to_all | solution.py:262
  24.7 1.8 %statistic.1 = (f32[512,256]{1,0:T(8,128)}, f32[8,16,128]{2,1,0:T(8,128)S(1)}) custom-call(bf16[512,128]{1,0:T(8,128)(2,1)S(1)} %bitcast.7, bf16[512,512]{1,0:T(8,128)(2,1)S(1)} %get-tuple-element.28.mask_ref, f32[512,128]{1,0:T(8,128)S(1)} %get-tuple-element.29.weigh_ref, f32[512,128]{1,0:T(8,128)S(1)} %get-tuple-element.30.coef_ref, ...), custom_call_target="tpu_custom_call" | custom-call | flops 400000000 | bytes 4000000 | tf_op jit(solution)/shard_map/statistic/pallas_call | solution.py:241
  26.5 8.6 %all_to_all.16 = f32[8,16,128]{2,1,0:T(8,128)S(1)} all-to-all(f32[8,16,128]{2,1,0:T(8,128)S(1)} %get-tuple-element.33), channel_id=1, replica_groups={{8,2,4,6,0,10,12,14},{9,3,5,7,1,11,13,15},{24,18,20,22,16,26,28,30},{25..., dimensions={0} | all-to-all | bytes 131072 | tf_op jit(solution)/shard_map/all_to_all | solution.py:262
  35.1 0.6 %slice_reduce_fusion = f32[16,32]{1,0:T(8,128)} fusion(f32[8,16,128]{2,1,0:T(8,128)S(1)} %all_to_all.16), kind=kLoop, calls=%fused_computation | loop fusion | flops 3584 | bytes 18432 | tf_op jit(solution)/shard_map/reduce_max | solution.py:280
Async XLA Ops:
  1.9 12.0 %all-to-all-start = ((s32[8,2,256]{2,1,0:T(2,128)}), s32[8,2,256]{2,1,0:T(2,128)S(1)}, u32[]{:S(2)}, u32[]{:S(2)}) async-start(s32[8,2,256]{2,1,0:T(2,128)} %broadcast_in_dim.6), calls=%async_computation | async-start | bytes 32768 | tf_op jit(solution)/shard_map/all_to_all | solution.py:262
  9.8 1.6 %copy-start = (bf16[32,4,8192]{2,1,0:T(4,128)(2,1)S(1)}, bf16[32,4,8192]{2,1,0:T(4,128)(2,1)}, u32[]{:S(2)}) copy-start(bf16[32,4,8192]{2,1,0:T(4,128)(2,1)} %spec_ref.1) | copy-start | bytes 6291460
  11.4 0.7 %copy-start.4 = (s32[32]{0:T(128)S(1)}, s32[32]{0:T(128)}, u32[]{:S(2)}) copy-start(s32[32]{0:T(128)} %param.10) | copy-start | bytes 388
  11.4 0.7 %copy-start.1 = (f32[512,4]{0,1:T(4,128)S(1)}, f32[512,4]{0,1:T(4,128)}, u32[]{:S(2)}) copy-start(f32[512,4]{0,1:T(4,128)} %param.9) | copy-start | bytes 24580
  11.4 0.7 %copy-start.2 = (f32[256]{0:T(256)S(1)}, f32[256]{0:T(256)}, u32[]{:S(2)}) copy-start(f32[256]{0:T(256)} %param.8) | copy-start | bytes 3076
  11.4 0.7 %copy-start.3 = (s32[32]{0:T(128)S(1)}, s32[32]{0:T(128)}, u32[]{:S(2)}) copy-start(s32[32]{0:T(128)} %durations_ref) | copy-start | bytes 388

commit v4 on v3

--- a/solution.py
+++ b/solution.py
@@ -207,9 +207,6 @@
     sums = sums - jnp.where(iota(sums.shape, 1) < half, 0.0, coef_ref[...]) * pltpu.roll(sums, half, 1)
     parts = jnp.concatenate(split(sums, 2), axis=1)
     found_ref[...] = jnp.dot(parts, block_ref[...], preferred_element_type=jnp.float32)
-    rows = map_ref.shape[0] // loudest_ref.shape[1]
-    copies = loudest_ref.shape[0]
-    per_step = LANES // rows
     leaving = []
     for step in range(map_ref.shape[0] // LANES):
         here = pl.ds(step * LANES, LANES)
@@ -224,38 +221,59 @@
         leaving.append(pltpu.make_async_copy(tile_ref.at[here, :], map_ref.at[here, :], sems.at[step]))
         leaving[-1].start()
         best = jnp.max(jnp.transpose(best), axis=0, keepdims=True)
-        for n in range(per_step):
-            turned = best if n == 0 else pltpu.roll(best, LANES - n * rows, 1)
-            loudest_ref[0, pl.ds(step * per_step + n, 1), :] = turned
-    for copy in range(1, copies):
-        loudest_ref[copy] = loudest_ref[0]
+        for copy in range(loudest_ref.shape[0]):
+            loudest_ref[copy, pl.ds(step, 1), :] = best
     for copy in leaving:
         copy.wait()
 
 
-def statistic(windows, mask, weigh, coef, kernel, rows, copies):
-    count = mask.shape[0] // rows
+def statistic(windows, mask, weigh, coef, kernel, copies):
+    total = mask.shape[0]
     templates = kernel.shape[1]
     features = 4 * W * (templates // LANES)
     vmem = pl.BlockSpec(memory_space=pltpu.VMEM)
     return pl.pallas_call(
         statistic_kernel,
         out_shape=(
-            jax.ShapeDtypeStruct((count * rows, templates), jnp.float32),
-            jax.ShapeDtypeStruct((copies, count, LANES), jnp.float32),
+            jax.ShapeDtypeStruct((total, templates), jnp.float32),
+            jax.ShapeDtypeStruct((copies, total // LANES, LANES), jnp.float32),
         ),
         in_specs=[vmem] * 5,
         out_specs=(pl.BlockSpec(memory_space=pl.ANY), vmem),
         scratch_shapes=[
             pltpu.VMEM((2 * features, 4 * templates), jnp.bfloat16),
-            pltpu.VMEM((count * rows, 4 * templates), jnp.float32),
-            pltpu.VMEM((count * rows, templates), jnp.float32),
-            pltpu.SemaphoreType.DMA((count * rows // LANES,)),
+            pltpu.VMEM((total, 4 * templates), jnp.float32),
+            pltpu.VMEM((total, templates), jnp.float32),
+            pltpu.SemaphoreType.DMA((total // LANES,)),
         ],
         compiler_params=pltpu.CompilerParams(vmem_limit_bytes=16 * 1024 * 1024),
         cost_estimate=pl.CostEstimate(flops=400_000_000, bytes_accessed=4_000_000, transcendentals=0),
         name="statistic",
     )(windows, mask, weigh, coef, kernel)
+
+
+def loudest_kernel(found_ref, out_ref):
+    best = found_ref[0]
+    for n in range(1, found_ref.shape[0]):
+        best = jnp.maximum(best, found_ref[n])
+    width = out_ref.shape[1]
+    for row in range(out_ref.shape[0]):
+        start = row * width
+        line = best[start // LANES : start // LANES + 1]
+        line = pltpu.roll(line, LANES - start % LANES, 1) if start % LANES else line
+        out_ref[row : row + 1, :] = line[:, :width]
+
+
+def largest(found, count, width):
+    vmem = pl.BlockSpec(memory_space=pltpu.VMEM)
+    return pl.pallas_call(
+        loudest_kernel,
+        out_shape=jax.ShapeDtypeStruct((count, width), jnp.float32),
+        in_specs=[vmem],
+        out_specs=vmem,
+        compiler_params=pltpu.CompilerParams(vmem_limit_bytes=8 * 1024 * 1024),
+        name="largest",
+    )(found)
 
 
 def exchange(values, axis, members):
@@ -276,8 +294,8 @@
     held, *prepared = lax.optimization_barrier((held, *prepared))
     windows = pick(known, held, by_band, [run % bands for run in by_run])
     arrived = exchange(windows.reshape(cores * bands, sft_rows, LANES), ("tm", "tmpl"), by_run)
-    fstat_map, loudest = statistic(arrived.reshape(-1, LANES), *prepared, grid_size, bands)
-    loudest = jnp.max(exchange(loudest, "tmpl", by_band)[:, :, :grid_size], axis=0)
+    fstat_map, loudest = statistic(arrived.reshape(-1, LANES), *prepared, bands)
+    loudest = largest(exchange(loudest, "tmpl", by_band), my_rows, grid_size)
     return (fstat_map.reshape(my_rows, grid_size, -1), loudest)
 
 

time: 36.1 us -> 35.9 us (level)
  Pallas kernels: 4.62 us -> 5.3 us
  other arithmetic: 0.61 us -> 0 us
    pallas_call x1 -> x2, Pallas kernels: 1.8 us -> 2.49 us  [the longest x1 1.8 us: statistic(): pl.pallas_call(statistic_kernel, out_shape=(jax.ShapeDtypeStruct((total,...]
    reduce_max x1 -> x0, other arithmetic: 0.61 us -> none  [body(): jnp.max(exchange(loudest, 'tmpl', by_band)[:, :, :grid_size], axis=0)]
where the time goes in v4:
time: 35.9 us; the launch traced here: 35.5 us
  blocking collectives  17.6 us (49%)
  starting transfers between devices  7.84 us (22%)
  Pallas kernels  5.3 us (15%)
  local copies, waits for them, and re-layouts  3.45 us (10%)
  waiting for transfers between devices  0.7 us (2%)
  between operations  0.67 us (2%)
    all_to_all x2, blocking collectives, exchange(): lax.all_to_all(values, axis, split_axis=0, concat_axis=0, axis_index_grou...  17.6 us
    all_to_all x1, starting transfers between devices, exchange(): lax.all_to_all(values, axis, split_axis=0, concat_axis=0, axis_index_grou...  7.84 us
    unnamed x10, local copies, waits for them, and re-layouts  2.09 us
    pallas_call x1, Pallas kernels, statistic(): pl.pallas_call(statistic_kernel, out_shape=(jax.ShapeDtypeStruct((total,...  1.8 us
    pallas_call x1, Pallas kernels, pick(): pl.pallas_call(functools.partial(pick_kernel, bands_in, bands_out), out_s...  1.5 us
    broadcast_in_dim x1, local copies, waits for them, and re-layouts, body(): jnp.broadcast_to(offsets.T[None], (bands,) + offsets.T.shape)  1.29 us
    pallas_call x1, Pallas kernels, prepare(): pl.pallas_call(functools.partial(prepare_kernel, first, run), out_shape=(...  1.16 us
  transfers between devices with their start and end apart: 1, of which 1 were waited for; matrix products, arithmetic and copies ran while one was open for 0% of the time, Pallas kernels for 4%

profile of v4, /device:TPU:0, one launch (start us, length us, event | category | flops | bytes accessed | tf_op | source)
XLA Modules:
  0.0 35.5 jit_solution(7115180344026101489)
XLA Ops:
  0.6 1.3 %broadcast_in_dim.6 = s32[8,2,256]{2,1,0:T(2,128)} broadcast(s32[2,256]{1,0:T(2,128)} %bitcast.10), dimensions={1,2} | broadcast | bytes 18432 | tf_op jit(solution)/shard_map/broadcast_in_dim | solution.py:291
  1.9 7.8 %all-to-all-start = ((s32[8,2,256]{2,1,0:T(2,128)}), s32[8,2,256]{2,1,0:T(2,128)S(1)}, u32[]{:S(2)}, u32[]{:S(2)}) async-start(s32[8,2,256]{2,1,0:T(2,128)} %broadcast_in_dim.6), calls=%async_computation | async-start | bytes 32768 | tf_op jit(solution)/shard_map/all_to_all | solution.py:280
  9.8 0.0 copy-start
  9.8 1.6 %copy-done = bf16[32,4,8192]{2,1,0:T(4,128)(2,1)S(1)} copy-done((bf16[32,4,8192]{2,1,0:T(4,128)(2,1)S(1)}, bf16[32,4,8192]{2,1,0:T(4,128)(2,1)}, u32[]{:S(2)}) %copy-start) | copy-done | bytes 2097176
  11.4 0.0 copy-start.4
  11.4 0.0 copy-start.1
  11.4 0.0 copy-start.2
  11.4 0.0 copy-start.3
  11.4 0.2 hold.1.spec_ref
  11.5 0.5 %copy-done.4 = s32[32]{0:T(128)S(1)} copy-done((s32[32]{0:T(128)S(1)}, s32[32]{0:T(128)}, u32[]{:S(2)}) %copy-start.4) | copy-done | bytes 152
  12.0 0.1 broadcast_in_dim.7.starts_ref
  12.1 0.0 copy-done.1
  12.1 0.0 copy-done.2
  12.1 0.0 copy-done.3
  12.1 1.2 %prepare.1 = (bf16[512,512]{1,0:T(8,128)(2,1)S(1)}, f32[512,128]{1,0:T(8,128)S(1)}, f32[512,128]{1,0:T(8,128)S(1)}, bf16[16,256]{1,0:T(8,128)(2,1)S(1)}) custom-call(s32[32]{0:T(128)S(1)} %copy-done.3, s32[32,128]{1,0:T(8,128)S(1)} %broadcast_in_dim.7.starts_ref, f32[4,512]{1,0:T(4,128)S(1)} %bitcast.8, f32[1,256]{1,0:T(1,128)S(1)} %bitcast.9), custom_call_target="tpu_custom_call" | custom-call | flops 100000000 | bytes 4000000 | tf_op jit(solution)/shard_map/prepare/pallas_call | solution.py:174
  13.3 0.7 %all-to-all-done.offset_ref = s32[8,2,256]{2,1,0:T(2,128)S(1)} async-done(((s32[8,2,256]{2,1,0:T(2,128)}), s32[8,2,256]{2,1,0:T(2,128)S(1)}, u32[]{:S(2)}, u32[]{:S(2)}) %all-to-all-start) | async-done | bytes 16416 | tf_op jit(solution)/shard_map/all_to_all | solution.py:280
  14.0 1.5 %pick.1 = bf16[512,128]{1,0:T(8,128)(2,1)S(1)} custom-call(s32[8,2,256]{2,1,0:T(2,128)S(1)} %all-to-all-done.offset_ref, bf16[32,4,8192]{2,1,0:T(4,128)(2,1)S(1)} %hold.1.spec_ref), custom_call_target="tpu_custom_call" | custom-call | flops 10000000 | bytes 2097152 | tf_op jit(solution)/shard_map/pick/pallas_call | solution.py:111
  15.5 9.3 %all_to_all.15 = bf16[16,32,128]{2,1,0:T(8,128)(2,1)S(1)} all-to-all(bf16[16,32,128]{2,1,0:T(8,128)(2,1)S(1)} %bitcast.6), channel_id=1, replica_groups={{9,2,4,6,8,10,12,14,1,3,5,7,0,11,13,15},{25,18,20,22,24,26,28,30,17,19,..., dimensions={0} | all-to-all | bytes 262144 | tf_op jit(solution)/shard_map/all_to_all | solution.py:280
  24.7 1.8 %statistic.1 = (f32[512,256]{1,0:T(8,128)}, f32[8,4,128]{2,1,0:T(4,128)S(1)}) custom-call(bf16[512,128]{1,0:T(8,128)(2,1)S(1)} %bitcast.7, bf16[512,512]{1,0:T(8,128)(2,1)S(1)} %get-tuple-element.28.mask_ref, f32[512,128]{1,0:T(8,128)S(1)} %get-tuple-element.29.weigh_ref, f32[512,128]{1,0:T(8,128)S(1)} %get-tuple-element.30.coef_ref, ...), custom_call_target="tpu_custom_call" | custom-call | flops 400000000 | bytes 4000000 | tf_op jit(solution)/shard_map/statistic/pallas_call | solution.py:235
  26.5 8.3 %all_to_all.16.found_ref = f32[8,4,128]{2,1,0:T(4,128)S(1)} all-to-all(f32[8,4,128]{2,1,0:T(4,128)S(1)} %get-tuple-element.33), channel_id=1, replica_groups={{8,2,4,6,0,10,12,14},{9,3,5,7,1,11,13,15},{24,18,20,22,16,26,28,30},{25..., dimensions={0} | all-to-all | bytes 32768 | tf_op jit(solution)/shard_map/all_to_all | solution.py:280
  34.9 0.7 %largest.1 = f32[16,32]{1,0:T(8,128)} custom-call(f32[8,4,128]{2,1,0:T(4,128)S(1)} %all_to_all.16.found_ref), custom_call_target="tpu_custom_call" | custom-call | tf_op jit(solution)/shard_map/largest/pallas_call | solution.py:269
Async XLA Ops:
  1.9 12.0 %all-to-all-start = ((s32[8,2,256]{2,1,0:T(2,128)}), s32[8,2,256]{2,1,0:T(2,128)S(1)}, u32[]{:S(2)}, u32[]{:S(2)}) async-start(s32[8,2,256]{2,1,0:T(2,128)} %broadcast_in_dim.6), calls=%async_computation | async-start | bytes 32768 | tf_op jit(solution)/shard_map/all_to_all | solution.py:280
  9.8 1.6 %copy-start = (bf16[32,4,8192]{2,1,0:T(4,128)(2,1)S(1)}, bf16[32,4,8192]{2,1,0:T(4,128)(2,1)}, u32[]{:S(2)}) copy-start(bf16[32,4,8192]{2,1,0:T(4,128)(2,1)} %spec_ref.1) | copy-start | bytes 6291460
  11.4 0.7 %copy-start.4 = (s32[32]{0:T(128)S(1)}, s32[32]{0:T(128)}, u32[]{:S(2)}) copy-start(s32[32]{0:T(128)} %param.10) | copy-start | bytes 388
  11.4 0.7 %copy-start.1 = (f32[512,4]{0,1:T(4,128)S(1)}, f32[512,4]{0,1:T(4,128)}, u32[]{:S(2)}) copy-start(f32[512,4]{0,1:T(4,128)} %param.9) | copy-start | bytes 24580
  11.4 0.7 %copy-start.2 = (f32[256]{0:T(256)S(1)}, f32[256]{0:T(256)}, u32[]{:S(2)}) copy-start(f32[256]{0:T(256)} %param.8) | copy-start | bytes 3076
  11.4 0.7 %copy-start.3 = (s32[32]{0:T(128)S(1)}, s32[32]{0:T(128)}, u32[]{:S(2)}) copy-start(s32[32]{0:T(128)} %durations_ref) | copy-start | bytes 388

commit v5 on v4

--- a/solution.py
+++ b/solution.py
@@ -65,7 +65,7 @@
     source = lane_group * (bands * blocks) + lane // W % blocks
     for band in range(bands):
         for pair in range(4):
-            place = jnp.take_along_axis(places[pair * 8 : pair * 8 + 8], source + band * blocks, axis=1, mode="promise_in_bounds")
+            place = jnp.take_along_axis(places[pair * 8 : pair * 8 + 8], (source + band * blocks) & (LANES - 1), axis=1, mode="promise_in_bounds")
             place_ref[band, pair] = place + ((lane & (W - 1)) + lane_group * band_width)
 
     def gather(band):

time: 35.9 us -> 35.9 us (level)
  no operation moved by 1% of the time
where the time goes in v5:
time: 35.9 us; the launch traced here: 35.5 us
  blocking collectives  17.6 us (49%)
  starting transfers between devices  7.84 us (22%)
  Pallas kernels  5.3 us (15%)
  local copies, waits for them, and re-layouts  3.45 us (10%)
  waiting for transfers between devices  0.7 us (2%)
  between operations  0.67 us (2%)
    all_to_all x2, blocking collectives, exchange(): lax.all_to_all(values, axis, split_axis=0, concat_axis=0, axis_index_grou...  17.6 us
    all_to_all x1, starting transfers between devices, exchange(): lax.all_to_all(values, axis, split_axis=0, concat_axis=0, axis_index_grou...  7.84 us
    unnamed x10, local copies, waits for them, and re-layouts  2.09 us
    pallas_call x1, Pallas kernels, statistic(): pl.pallas_call(statistic_kernel, out_shape=(jax.ShapeDtypeStruct((total,...  1.8 us
    pallas_call x1, Pallas kernels, pick(): pl.pallas_call(functools.partial(pick_kernel, bands_in, bands_out), out_s...  1.5 us
    broadcast_in_dim x1, local copies, waits for them, and re-layouts, body(): jnp.broadcast_to(offsets.T[None], (bands,) + offsets.T.shape)  1.29 us
    pallas_call x1, Pallas kernels, prepare(): pl.pallas_call(functools.partial(prepare_kernel, first, run), out_shape=(...  1.16 us
  transfers between devices with their start and end apart: 1, of which 1 were waited for; matrix products, arithmetic and copies ran while one was open for 0% of the time, Pallas kernels for 4%

profile of v5, /device:TPU:0, one launch (start us, length us, event | category | flops | bytes accessed | tf_op | source)
XLA Modules:
  0.0 35.5 jit_solution(9254585269807456520)
XLA Ops:
  0.6 1.3 %broadcast_in_dim.6 = s32[8,2,256]{2,1,0:T(2,128)} broadcast(s32[2,256]{1,0:T(2,128)} %bitcast.10), dimensions={1,2} | broadcast | bytes 18432 | tf_op jit(solution)/shard_map/broadcast_in_dim | solution.py:291
  1.9 7.8 %all-to-all-start = ((s32[8,2,256]{2,1,0:T(2,128)}), s32[8,2,256]{2,1,0:T(2,128)S(1)}, u32[]{:S(2)}, u32[]{:S(2)}) async-start(s32[8,2,256]{2,1,0:T(2,128)} %broadcast_in_dim.6), calls=%async_computation | async-start | bytes 32768 | tf_op jit(solution)/shard_map/all_to_all | solution.py:280
  9.8 0.0 copy-start
  9.8 1.6 %copy-done = bf16[32,4,8192]{2,1,0:T(4,128)(2,1)S(1)} copy-done((bf16[32,4,8192]{2,1,0:T(4,128)(2,1)S(1)}, bf16[32,4,8192]{2,1,0:T(4,128)(2,1)}, u32[]{:S(2)}) %copy-start) | copy-done | bytes 2097176
  11.4 0.0 copy-start.4
  11.4 0.0 copy-start.1
  11.4 0.0 copy-start.2
  11.4 0.0 copy-start.3
  11.4 0.2 hold.1.spec_ref
  11.5 0.5 %copy-done.4 = s32[32]{0:T(128)S(1)} copy-done((s32[32]{0:T(128)S(1)}, s32[32]{0:T(128)}, u32[]{:S(2)}) %copy-start.4) | copy-done | bytes 152
  12.0 0.1 broadcast_in_dim.7.starts_ref
  12.1 0.0 copy-done.1
  12.1 0.0 copy-done.2
  12.1 0.0 copy-done.3
  12.1 1.2 %prepare.1 = (bf16[512,512]{1,0:T(8,128)(2,1)S(1)}, f32[512,128]{1,0:T(8,128)S(1)}, f32[512,128]{1,0:T(8,128)S(1)}, bf16[16,256]{1,0:T(8,128)(2,1)S(1)}) custom-call(s32[32]{0:T(128)S(1)} %copy-done.3, s32[32,128]{1,0:T(8,128)S(1)} %broadcast_in_dim.7.starts_ref, f32[4,512]{1,0:T(4,128)S(1)} %bitcast.8, f32[1,256]{1,0:T(1,128)S(1)} %bitcast.9), custom_call_target="tpu_custom_call" | custom-call | flops 100000000 | bytes 4000000 | tf_op jit(solution)/shard_map/prepare/pallas_call | solution.py:174
  13.3 0.7 %all-to-all-done.offset_ref = s32[8,2,256]{2,1,0:T(2,128)S(1)} async-done(((s32[8,2,256]{2,1,0:T(2,128)}), s32[8,2,256]{2,1,0:T(2,128)S(1)}, u32[]{:S(2)}, u32[]{:S(2)}) %all-to-all-start) | async-done | bytes 16416 | tf_op jit(solution)/shard_map/all_to_all | solution.py:280
  14.0 1.5 %pick.1 = bf16[512,128]{1,0:T(8,128)(2,1)S(1)} custom-call(s32[8,2,256]{2,1,0:T(2,128)S(1)} %all-to-all-done.offset_ref, bf16[32,4,8192]{2,1,0:T(4,128)(2,1)S(1)} %hold.1.spec_ref), custom_call_target="tpu_custom_call" | custom-call | flops 10000000 | bytes 2097152 | tf_op jit(solution)/shard_map/pick/pallas_call | solution.py:111
  15.5 9.3 %all_to_all.15 = bf16[16,32,128]{2,1,0:T(8,128)(2,1)S(1)} all-to-all(bf16[16,32,128]{2,1,0:T(8,128)(2,1)S(1)} %bitcast.6), channel_id=1, replica_groups={{9,2,4,6,8,10,12,14,1,3,5,7,0,11,13,15},{25,18,20,22,24,26,28,30,17,19,..., dimensions={0} | all-to-all | bytes 262144 | tf_op jit(solution)/shard_map/all_to_all | solution.py:280
  24.7 1.8 %statistic.1 = (f32[512,256]{1,0:T(8,128)}, f32[8,4,128]{2,1,0:T(4,128)S(1)}) custom-call(bf16[512,128]{1,0:T(8,128)(2,1)S(1)} %bitcast.7, bf16[512,512]{1,0:T(8,128)(2,1)S(1)} %get-tuple-element.28.mask_ref, f32[512,128]{1,0:T(8,128)S(1)} %get-tuple-element.29.weigh_ref, f32[512,128]{1,0:T(8,128)S(1)} %get-tuple-element.30.coef_ref, ...), custom_call_target="tpu_custom_call" | custom-call | flops 400000000 | bytes 4000000 | tf_op jit(solution)/shard_map/statistic/pallas_call | solution.py:235
  26.5 8.3 %all_to_all.16.found_ref = f32[8,4,128]{2,1,0:T(4,128)S(1)} all-to-all(f32[8,4,128]{2,1,0:T(4,128)S(1)} %get-tuple-element.33), channel_id=1, replica_groups={{8,2,4,6,0,10,12,14},{9,3,5,7,1,11,13,15},{24,18,20,22,16,26,28,30},{25..., dimensions={0} | all-to-all | bytes 32768 | tf_op jit(solution)/shard_map/all_to_all | solution.py:280
  34.9 0.7 %largest.1 = f32[16,32]{1,0:T(8,128)} custom-call(f32[8,4,128]{2,1,0:T(4,128)S(1)} %all_to_all.16.found_ref), custom_call_target="tpu_custom_call" | custom-call | tf_op jit(solution)/shard_map/largest/pallas_call | solution.py:269
Async XLA Ops:
  1.9 12.0 %all-to-all-start = ((s32[8,2,256]{2,1,0:T(2,128)}), s32[8,2,256]{2,1,0:T(2,128)S(1)}, u32[]{:S(2)}, u32[]{:S(2)}) async-start(s32[8,2,256]{2,1,0:T(2,128)} %broadcast_in_dim.6), calls=%async_computation | async-start | bytes 32768 | tf_op jit(solution)/shard_map/all_to_all | solution.py:280
  9.8 1.6 %copy-start = (bf16[32,4,8192]{2,1,0:T(4,128)(2,1)S(1)}, bf16[32,4,8192]{2,1,0:T(4,128)(2,1)}, u32[]{:S(2)}) copy-start(bf16[32,4,8192]{2,1,0:T(4,128)(2,1)} %spec_ref.1) | copy-start | bytes 6291460
  11.4 0.7 %copy-start.4 = (s32[32]{0:T(128)S(1)}, s32[32]{0:T(128)}, u32[]{:S(2)}) copy-start(s32[32]{0:T(128)} %param.10) | copy-start | bytes 388
  11.4 0.7 %copy-start.1 = (f32[512,4]{0,1:T(4,128)S(1)}, f32[512,4]{0,1:T(4,128)}, u32[]{:S(2)}) copy-start(f32[512,4]{0,1:T(4,128)} %param.9) | copy-start | bytes 24580
  11.4 0.7 %copy-start.2 = (f32[256]{0:T(256)S(1)}, f32[256]{0:T(256)}, u32[]{:S(2)}) copy-start(f32[256]{0:T(256)} %param.8) | copy-start | bytes 3076
  11.4 0.7 %copy-start.3 = (s32[32]{0:T(128)S(1)}, s32[32]{0:T(128)}, u32[]{:S(2)}) copy-start(s32[32]{0:T(128)} %durations_ref) | copy-start | bytes 388
